TPU v7x, 32 devices: a whole 2x2x4 slice. The times are simulated.
32 devices in a mesh: gx: 8 (over y, x, core), gy: 4 (over z).
Axes of the slice: x: 2, y: 2, z: 4, core: 2. Of those that a mesh axis runs over, the one named last changes fastest.
Arguments:
- provisional: bfloat16 [4, 8, 1024, 1024], P(None, 'gx', 'gy'), may hold values from -6 to 6
- implicit_terms: bfloat16 [4, 8, 1024, 1024], P(None, 'gx', 'gy'), may hold values from -6 to 6
- adv_speed: float32 [8, 1024], P('gx'), may hold values from 0.2 to 1.2
- reaction: float32 [8, 1024], P('gx'), may hold values from 0.1 to 2
- wall_rate: float32 [1024], replicated, may hold values from 0.05 to 20
- span_rate: float32 [1024], replicated, may hold values from 0.01 to 4
- analysis: bfloat16 [1024, 1024], replicated, may hold values from -1 to 2
- synthesis: bfloat16 [1024, 1024], replicated, may hold values from -1 to 2
Outputs:
- end_value: float32 [8, 1024, 1024], P('gx', 'gy')
All inputs are finite; a program needn't handle non-finite values.
Results may differ from a plain program's by a relative error of at most 0.0063.
Values may be sent and summed in bfloat16 or wider, within the bound.
A program may use at most 64 MiB of HBM per device.

v0:
```python
import math
import jax
import jax.numpy as jnp
from jax import lax
from jax.sharding import PartitionSpec as P


def extended(cells, sides, width):
    for axis, dim in sides:
        count = lax.axis_size(axis)
        head = lax.slice_in_dim(cells, 0, width, axis=dim)
        tail = lax.slice_in_dim(cells, cells.shape[dim] - width, cells.shape[dim], axis=dim)
        cells = jnp.concatenate(
            [
                lax.ppermute(tail, axis, [(i, (i + 1) % count) for i in range(count)]),
                cells,
                lax.ppermute(head, axis, [((i + 1) % count, i) for i in range(count)]),
            ],
            axis=dim,
        )
    return cells


def spectral_weights():
    root_five = math.sqrt(5.0)
    points = [0.0, 0.5 - 0.5 / root_five, 0.5 + 0.5 / root_five, 1.0]
    gauss_offset = 1.0 / math.sqrt(3.0)
    weights = [[0.0, 0.0, 0.0, 0.0] for m in range(3)]
    for m in range(3):
        half_width = 0.5 * (points[m + 1] - points[m])
        centre = 0.5 * (points[m + 1] + points[m])
        for sign_factor in (-1.0, 1.0):
            sample = centre + half_width * sign_factor * gauss_offset
            for j in range(4):
                basis_value = 1.0
                for i in range(4):
                    if i != j:
                        basis_value = basis_value * (sample - points[i]) / (points[j] - points[i])
                weights[m][j] = weights[m][j] + half_width * basis_value
    return (points, weights)


def explicit_term(values, velocity, decay_rate):
    padded = extended(values, (("gx", 1),), 1)
    forward = padded[:, 2:].astype(jnp.float32)
    behind = padded[:, :-2].astype(jnp.float32)
    return -velocity * (forward - behind) * 0.5 - decay_rate * values.astype(jnp.float32)


def wall_solve(rhs_block, analysis, synthesis, factors):
    coefficients = jnp.einsum(
        "ij,xjk->xik", analysis, rhs_block, preferred_element_type=jnp.float32
    )
    scaled = (coefficients * factors).astype(jnp.bfloat16)
    return jnp.einsum("ji,xik->xjk", synthesis, scaled, preferred_element_type=jnp.float32)


def per_device(
    provisional, implicit_terms, adv_speed, reaction, wall_rate, span_rate, analysis, synthesis
):
    points, weights = spectral_weights()
    modes_dev = span_rate.shape[0] // lax.axis_size("gy")
    span_part = lax.dynamic_slice_in_dim(span_rate, lax.axis_index("gy") * modes_dev, modes_dev, 0)
    rows_dev = provisional.shape[2]
    row_start = lax.axis_index("gy") * rows_dev
    velocity = lax.dynamic_slice_in_dim(adv_speed, row_start, rows_dev, 1)[None, :, :, None]
    decay_rate = lax.dynamic_slice_in_dim(reaction, row_start, rows_dev, 1)[None, :, :, None]
    old_explicit = explicit_term(provisional, velocity, decay_rate)
    sources = old_explicit + implicit_terms.astype(jnp.float32)
    current = provisional[0].astype(jnp.float32)
    new_explicit = old_explicit[0]
    for m in range(3):
        step_size = float(points[m + 1] - points[m])
        quadrature = float(weights[m][0]) * sources[0]
        for j in range(1, 4):
            quadrature = quadrature + float(weights[m][j]) * sources[j]
        rhs = (
            current
            + step_size * (new_explicit - old_explicit[m])
            - step_size * implicit_terms[m + 1].astype(jnp.float32)
            + quadrature
        )
        rounded = rhs.astype(jnp.bfloat16)
        factors = 1.0 / (1.0 + step_size * (wall_rate[:, None] + span_part[None, :]))
        solved = wall_solve(
            lax.all_to_all(rounded, "gy", split_axis=2, concat_axis=1, tiled=True),
            analysis,
            synthesis,
            factors,
        )
        current = lax.all_to_all(solved, "gy", split_axis=1, concat_axis=2, tiled=True)
        if m < 2:
            new_explicit = explicit_term(current.astype(jnp.bfloat16)[None], velocity, decay_rate)[
                0
            ]
    return current


def solution(mesh):
    placed = (
        P(None, "gx", "gy", None),
        P(None, "gx", "gy", None),
        P("gx", None),
        P("gx", None),
        P(),
        P(),
        P(),
        P(),
    )
    return jax.shard_map(
        per_device, mesh=mesh, in_specs=placed, out_specs=P("gx", "gy", None), check_vma=False
    )
```

profile of v0, /device:TPU:0, one launch (start us, length us, event | category | flops | bytes accessed | tf_op | source)
XLA Modules:
  0.0 308.2 jit_solution(4075768437817554544)
XLA Ops:
  0.0 3.3 %collective-permute-start = (bf16[4,1,256,1024]{3,2,1,0:T(8,128)(2,1)}, bf16[4,1,256,1024]{3,2,1,0:T(8,128)(2,1)}, u32[]{:S(2)}, u32[]{:S(2)}) collective-permute-start(bf16[4,1,256,1024]{3,2,1,0:T(8,128)(2,1)} %param.8), channel_id=1, source_target_pairs={{4,0},{8,4},{12,8},{16,12},{20,16},{24,20},{28,24},{0,28},{5,1},{9... | collective-permute-start | bytes 6291464 | tf_op jit(solution)/shard_map/ppermute | solution.py:17
  4.0 44.7 %collective-permute-done = bf16[4,1,256,1024]{3,2,1,0:T(8,128)(2,1)} collective-permute-done((bf16[4,1,256,1024]{3,2,1,0:T(8,128)(2,1)}, bf16[4,1,256,1024]{3,2,1,0:T(8,128)(2,1)}, u32[]{:S(2)}, u32[]{:S(2)}) %collective-permute-start) | collective-permute-done | bytes 2097184 | tf_op jit(solution)/shard_map/ppermute | solution.py:17
  50.7 5.7 %convert_add_fusion = (f32[4,1,256,1024]{3,2,1,0:T(8,128)S(1)}, f32[4,1,256,1024]{3,2,1,0:T(8,128)S(1)}) fusion(bf16[4,1,256,1024]{3,2,1,0:T(8,128)(2,1)} %param.9, bf16[4,1,256,1024]{3,2,1,0:T(8,128)(2,1)} %param.8, f32[256]{0:T(256)S(1)} %bitcast.160, bf16[4,1,256,1024]{3,2,1,0:T(8,128)(2,1)} %collective-permute-done.1, ...), kind=kLoop, calls=%fused_computation | loop fusion | flops 10485760 | bytes 16779264 | tf_op jit(solution)/shard_map/add | solution.py:69
  59.6 2.8 fusion.42
  62.3 2.4 copy.54
  65.2 4.5 %reduce = bf16[1024,256]{1,0:T(8,128)(2,1)} reduce(bf16[1024,1,256]{2,1,0:T(2,128)(2,1)S(1)} %bitcast.143, bf16[]{:T(256)} %broadcast.416), dimensions={1}, to_apply=%bitcast.117.reduce_sub_computation | reduce | bytes 1048578
  71.8 4.9 %all-to-all-start = ((bf16[4,2,32768]{2,1,0:T(2,128)(2,1)}), bf16[4,2,32768]{2,1,0:T(2,128)(2,1)}, u32[]{:S(2)}, u32[]{:S(2)}) async-start(bf16[4,2,32768]{2,1,0:T(2,128)(2,1)} %reshape.671), calls=%async_computation | async-start | bytes 1048576 | tf_op jit(solution)/shard_map/all_to_all | solution.py:86
  77.4 11.3 %all-to-all-done = bf16[4,2,32768]{2,1,0:T(2,128)(2,1)} async-done(((bf16[4,2,32768]{2,1,0:T(2,128)(2,1)}), bf16[4,2,32768]{2,1,0:T(2,128)(2,1)}, u32[]{:S(2)}, u32[]{:S(2)}) %all-to-all-start) | async-done | bytes 524320 | tf_op jit(solution)/shard_map/all_to_all | solution.py:86
  88.7 2.2 reshape.672
  93.9 3.2 %convolution_bitcast_fusion.4 = f32[1,1024,256]{1,2,0:T(8,128)S(1)} fusion(bf16[1024,1024]{1,0:T(8,128)(2,1)S(1)} %copy-done, bf16[1024,256]{1,0:T(8,128)(2,1)} %bitcast.155, bf16[1024,1024]{1,0:T(8,128)(2,1)} %param.14, f32[256]{0:T(256)S(1)} %dynamic_slice.11, f32[1024]{0:T(1024)S(1)} %copy-done.3), kind=kOutput, calls=%fused_computation.8 | convolution fusion | flops 1075314688 | bytes 5772288 | tf_op jit(solution)/shard_map/ji,xik->xjk/dot_general | solution.py:55
  99.0 27.0 %all_to_all.99 = f32[1,1024,256]{2,0,1:T(1,128)S(1)} all-to-all(f32[1,1024,256]{2,0,1:T(1,128)} %copy.56), channel_id=1, replica_groups=mesh['gx'=8,'gy'=4] {'gy'}, dimensions={1} | all-to-all | bytes 2097152 | tf_op jit(solution)/shard_map/all_to_all | solution.py:91
  127.4 2.2 convert_element_type.185
  129.6 4.0 %collective-permute-start.2 = (bf16[1,1,256,1024]{3,2,1,0:T(8,128)(2,1)}, bf16[1,1,256,1024]{3,2,1,0:T(8,128)(2,1)}, u32[]{:S(2)}, u32[]{:S(2)}) collective-permute-start(bf16[1,1,256,1024]{3,2,1,0:T(8,128)(2,1)} %convert_element_type.185), channel_id=1, source_target_pairs={{4,0},{8,4},{12,8},{16,12},{20,16},{24,20},{28,24},{0,28},{5,1},{9... | collective-permute-start | bytes 1572872 | tf_op jit(solution)/shard_map/ppermute | solution.py:17
  137.0 7.5 %collective-permute-done.2 = bf16[1,1,256,1024]{3,2,1,0:T(8,128)(2,1)} collective-permute-done((bf16[1,1,256,1024]{3,2,1,0:T(8,128)(2,1)}, bf16[1,1,256,1024]{3,2,1,0:T(8,128)(2,1)}, u32[]{:S(2)}, u32[]{:S(2)}) %collective-permute-start.2) | collective-permute-done | bytes 524320 | tf_op jit(solution)/shard_map/ppermute | solution.py:17
  144.5 4.0 %collective-permute-done.3 = bf16[1,1,256,1024]{3,2,1,0:T(8,128)(2,1)} collective-permute-done((bf16[1,1,256,1024]{3,2,1,0:T(8,128)(2,1)}, bf16[1,1,256,1024]{3,2,1,0:T(8,128)(2,1)}, u32[]{:S(2)}, u32[]{:S(2)}) %collective-permute-start.3) | collective-permute-done | bytes 524320 | tf_op jit(solution)/shard_map/ppermute | solution.py:15
  148.5 4.9 %fusion.24 = bf16[1,256,1024]{2,1,0:T(8,128)(2,1)} fusion(f32[1,256,1024]{2,1,0:T(8,128)S(1)} %all_to_all.78, f32[4,1,256,1024]{3,2,1,0:T(8,128)} %copy-done.2, bf16[1,1,256,1024]{3,2,1,0:T(8,128)(2,1)} %convert_element_type.185, bf16[1,1,256,1024]{3,2,1,0:T(8,128)(2,1)} %collective-permute-done.3, bf16[1,1,256,1024]{3,2,1,0:T(8,128)(2,1)} %collective-permute-done.2, ...), kind=kLoop, calls=%fused_computation.36 | loop fusion | flops 6029312 | bytes 8914944 | tf_op jit(solution)/shard_map/convert_element_type | solution.py:83
  153.3 2.4 copy.58
  155.7 4.5 %reduce.1 = bf16[1024,256]{1,0:T(8,128)(2,1)} reduce(bf16[1024,1,256]{2,1,0:T(2,128)(2,1)S(1)} %bitcast.146, bf16[]{:T(256)} %broadcast.416), dimensions={1}, to_apply=%bitcast.119.reduce_sub_computation | reduce | bytes 1048578
  161.4 17.3 %all_to_all.100 = bf16[4,2,32768]{2,1,0:T(2,128)(2,1)} all-to-all(bf16[4,2,32768]{2,1,0:T(2,128)(2,1)S(1)} %reshape.673), channel_id=1, replica_groups=mesh['gx'=8,'gy'=4] {'gy'}, dimensions={0} | all-to-all | bytes 1048576 | tf_op jit(solution)/shard_map/all_to_all | solution.py:86
  178.7 2.2 reshape.674
  183.9 3.2 %convolution_bitcast_fusion.2 = f32[1,1024,256]{1,2,0:T(8,128)S(1)} fusion(bf16[1024,1024]{1,0:T(8,128)(2,1)S(1)} %copy-done, bf16[1024,256]{1,0:T(8,128)(2,1)} %bitcast.156, bf16[1024,1024]{1,0:T(8,128)(2,1)} %param.14, f32[256]{0:T(256)S(1)} %dynamic_slice.11, f32[1024]{0:T(1024)S(1)} %copy-done.3), kind=kOutput, calls=%fused_computation.6 | convolution fusion | flops 1075314688 | bytes 5772288 | tf_op jit(solution)/shard_map/ji,xik->xjk/dot_general | solution.py:55
  189.0 28.3 %all_to_all.101 = f32[1,1024,256]{2,0,1:T(1,128)S(1)} all-to-all(f32[1,1024,256]{2,0,1:T(1,128)} %copy.60), channel_id=1, replica_groups=mesh['gx'=8,'gy'=4] {'gy'}, dimensions={1} | all-to-all | bytes 2097152 | tf_op jit(solution)/shard_map/all_to_all | solution.py:91
  218.7 2.2 convert_element_type.193
  224.9 6.0 %collective-permute-done.4 = bf16[1,1,256,1024]{3,2,1,0:T(8,128)(2,1)} collective-permute-done((bf16[1,1,256,1024]{3,2,1,0:T(8,128)(2,1)}, bf16[1,1,256,1024]{3,2,1,0:T(8,128)(2,1)}, u32[]{:S(2)}, u32[]{:S(2)}) %collective-permute-start.4) | collective-permute-done | bytes 524320 | tf_op jit(solution)/shard_map/ppermute | solution.py:17
  230.9 3.9 %collective-permute-done.5 = bf16[1,1,256,1024]{3,2,1,0:T(8,128)(2,1)} collective-permute-done((bf16[1,1,256,1024]{3,2,1,0:T(8,128)(2,1)}, bf16[1,1,256,1024]{3,2,1,0:T(8,128)(2,1)}, u32[]{:S(2)}, u32[]{:S(2)}) %collective-permute-start.5) | collective-permute-done | bytes 524320 | tf_op jit(solution)/shard_map/ppermute | solution.py:15
  234.8 4.9 %fusion.18 = bf16[1,256,1024]{2,1,0:T(8,128)(2,1)} fusion(f32[1,256,1024]{2,1,0:T(8,128)S(1)} %all_to_all.85, f32[4,1,256,1024]{3,2,1,0:T(8,128)} %copy-done.2, bf16[1,1,256,1024]{3,2,1,0:T(8,128)(2,1)} %convert_element_type.193, bf16[1,1,256,1024]{3,2,1,0:T(8,128)(2,1)} %collective-permute-done.5, bf16[1,1,256,1024]{3,2,1,0:T(8,128)(2,1)} %collective-permute-done.4, ...), kind=kLoop, calls=%fused_computation.29 | loop fusion | flops 6029312 | bytes 8914944 | tf_op jit(solution)/shard_map/convert_element_type | solution.py:83
  239.7 2.4 copy.62
  242.1 4.5 %reduce.2 = bf16[1024,256]{1,0:T(8,128)(2,1)} reduce(bf16[1024,1,256]{2,1,0:T(2,128)(2,1)S(1)} %bitcast.144, bf16[]{:T(256)} %broadcast.416), dimensions={1}, to_apply=%bitcast.121.reduce_sub_computation | reduce | bytes 1048578
  247.8 18.7 %all_to_all.102 = bf16[4,2,32768]{2,1,0:T(2,128)(2,1)} all-to-all(bf16[4,2,32768]{2,1,0:T(2,128)(2,1)S(1)} %reshape.675), channel_id=1, replica_groups=mesh['gx'=8,'gy'=4] {'gy'}, dimensions={0} | all-to-all | bytes 1048576 | tf_op jit(solution)/shard_map/all_to_all | solution.py:86
  270.9 4.0 %convolution_bitcast_fusion = f32[1,1024,256]{1,2,0:T(8,128)} fusion(bf16[1024,1024]{1,0:T(8,128)(2,1)S(1)} %copy-done, bf16[1024,256]{1,0:T(8,128)(2,1)S(1)} %bitcast.154, bf16[1024,1024]{1,0:T(8,128)(2,1)} %param.14, f32[256]{0:T(256)S(1)} %dynamic_slice.11, f32[1024]{0:T(1024)S(1)} %copy-done.3), kind=kOutput, calls=%fused_computation.4 | convolution fusion | flops 1075314688 | bytes 5772288 | tf_op jit(solution)/shard_map/ji,xik->xjk/dot_general | solution.py:55
  274.9 2.4 copy.64
  277.3 28.7 %all_to_all.103 = f32[1,1024,256]{2,0,1:T(1,128)S(1)} all-to-all(f32[1,1024,256]{2,0,1:T(1,128)S(1)} %copy.64), channel_id=1, replica_groups=mesh['gx'=8,'gy'=4] {'gy'}, dimensions={1} | all-to-all | bytes 2097152 | tf_op jit(solution)/shard_map/all_to_all | solution.py:91
  (36 shorter events, 37.9 us)
Async XLA Ops:
  0.0 93.9 %copy-start = (bf16[1024,1024]{1,0:T(8,128)(2,1)S(1)}, bf16[1024,1024]{1,0:T(8,128)(2,1)}, u32[]{:S(2)}) copy-start(bf16[1024,1024]{1,0:T(8,128)(2,1)} %param.15) | copy-start | bytes 6291460
  0.0 48.8 %collective-permute-start = (bf16[4,1,256,1024]{3,2,1,0:T(8,128)(2,1)}, bf16[4,1,256,1024]{3,2,1,0:T(8,128)(2,1)}, u32[]{:S(2)}, u32[]{:S(2)}) collective-permute-start(bf16[4,1,256,1024]{3,2,1,0:T(8,128)(2,1)} %param.8), channel_id=1, source_target_pairs={{4,0},{8,4},{12,8},{16,12},{20,16},{24,20},{28,24},{0,28},{5,1},{9... | collective-permute-start | bytes 6291464 | tf_op jit(solution)/shard_map/ppermute | solution.py:17
  3.3 47.4 %collective-permute-start.1 = (bf16[4,1,256,1024]{3,2,1,0:T(8,128)(2,1)}, bf16[4,1,256,1024]{3,2,1,0:T(8,128)(2,1)}, u32[]{:S(2)}, u32[]{:S(2)}) collective-permute-start(bf16[4,1,256,1024]{3,2,1,0:T(8,128)(2,1)} %param.8), channel_id=1, source_target_pairs={{0,4},{4,8},{8,12},{12,16},{16,20},{20,24},{24,28},{28,0},{1,5},{5... | collective-permute-start | bytes 6291464 | tf_op jit(solution)/shard_map/ppermute | solution.py:15
  56.4 2.0 copy-start.1
  56.4 3.2 %copy-start.2 = (f32[4,1,256,1024]{3,2,1,0:T(8,128)}, f32[4,1,256,1024]{3,2,1,0:T(8,128)S(1)}, u32[]{:S(2)}) copy-start(f32[4,1,256,1024]{3,2,1,0:T(8,128)S(1)} %get-tuple-element.6) | copy-start | bytes 12582916
  71.8 16.9 %all-to-all-start = ((bf16[4,2,32768]{2,1,0:T(2,128)(2,1)}), bf16[4,2,32768]{2,1,0:T(2,128)(2,1)}, u32[]{:S(2)}, u32[]{:S(2)}) async-start(bf16[4,2,32768]{2,1,0:T(2,128)(2,1)} %reshape.671), calls=%async_computation | async-start | bytes 1048576 | tf_op jit(solution)/shard_map/all_to_all | solution.py:86
  77.4 16.5 %copy-start.3 = (f32[1024]{0:T(1024)S(1)}, f32[1024]{0:T(1024)}, u32[]{:S(2)}) copy-start(f32[1024]{0:T(1024)} %param.12) | copy-start | bytes 12292
  129.6 14.9 %collective-permute-start.2 = (bf16[1,1,256,1024]{3,2,1,0:T(8,128)(2,1)}, bf16[1,1,256,1024]{3,2,1,0:T(8,128)(2,1)}, u32[]{:S(2)}, u32[]{:S(2)}) collective-permute-start(bf16[1,1,256,1024]{3,2,1,0:T(8,128)(2,1)} %convert_element_type.185), channel_id=1, source_target_pairs={{4,0},{8,4},{12,8},{16,12},{20,16},{24,20},{28,24},{0,28},{5,1},{9... | collective-permute-start | bytes 1572872 | tf_op jit(solution)/shard_map/ppermute | solution.py:17
  133.6 14.9 %collective-permute-start.3 = (bf16[1,1,256,1024]{3,2,1,0:T(8,128)(2,1)}, bf16[1,1,256,1024]{3,2,1,0:T(8,128)(2,1)}, u32[]{:S(2)}, u32[]{:S(2)}) collective-permute-start(bf16[1,1,256,1024]{3,2,1,0:T(8,128)(2,1)} %convert_element_type.185), channel_id=1, source_target_pairs={{0,4},{4,8},{8,12},{12,16},{16,20},{20,24},{24,28},{28,0},{1,5},{5... | collective-permute-start | bytes 1572872 | tf_op jit(solution)/shard_map/ppermute | solution.py:15
  221.0 9.9 %collective-permute-start.4 = (bf16[1,1,256,1024]{3,2,1,0:T(8,128)(2,1)}, bf16[1,1,256,1024]{3,2,1,0:T(8,128)(2,1)}, u32[]{:S(2)}, u32[]{:S(2)}) collective-permute-start(bf16[1,1,256,1024]{3,2,1,0:T(8,128)(2,1)} %convert_element_type.193), channel_id=1, source_target_pairs={{4,0},{8,4},{12,8},{16,12},{20,16},{24,20},{28,24},{0,28},{5,1},{9... | collective-permute-start | bytes 1572872 | tf_op jit(solution)/shard_map/ppermute | solution.py:17
  221.0 13.8 %collective-permute-start.5 = (bf16[1,1,256,1024]{3,2,1,0:T(8,128)(2,1)}, bf16[1,1,256,1024]{3,2,1,0:T(8,128)(2,1)}, u32[]{:S(2)}, u32[]{:S(2)}) collective-permute-start(bf16[1,1,256,1024]{3,2,1,0:T(8,128)(2,1)} %convert_element_type.193), channel_id=1, source_target_pairs={{0,4},{4,8},{8,12},{12,16},{16,20},{20,24},{24,28},{28,0},{1,5},{5... | collective-permute-start | bytes 1572872 | tf_op jit(solution)/shard_map/ppermute | solution.py:15
where the time goes:
time: 310 us; the launch traced here: 308 us
  blocking collectives  120 us (39%)
  waiting for transfers between devices  79.3 us (26%)
  local copies, waits for them, and re-layouts  53.3 us (17%)
  other arithmetic  32.4 us (10%)
  starting transfers between devices  12.7 us (4%)
  matrix products  10.4 us (3%)
    all_to_all x3, blocking collectives, per_device(): lax.all_to_all(solved, 'gy', split_axis=1, concat_axis=2, tiled=True)  83.9 us
    ppermute x3, waiting for transfers between devices, extended(): lax.ppermute(head, axis, [((i + 1) % count, i) for i in range(count)])  58.2 us
    all_to_all x2, blocking collectives, per_device(): lax.all_to_all(rounded, 'gy', split_axis=2, concat_axis=1, tiled=True)  36 us
    unnamed x18, local copies, waits for them, and re-layouts  17.3 us
    unnamed x3, other arithmetic  13.6 us
    convert_element_type x3, other arithmetic, per_device(): rounded = rhs.astype(jnp.bfloat16)  12.5 us
    all_to_all x8, local copies, waits for them, and re-layouts, per_device(): lax.all_to_all(solved, 'gy', split_axis=1, concat_axis=2, tiled=True)  11.9 us
    all_to_all x1, waiting for transfers between devices, per_device(): lax.all_to_all(rounded, 'gy', split_axis=2, concat_axis=1, tiled=True)  11.3 us
  transfers between devices with their start and end apart: 7, of which 7 were waited for; matrix products, arithmetic and copies ran while one was open for 2% of the time, Pallas kernels for 0%

commit v1 on v0

--- a/solution.py
+++ b/solution.py
@@ -3,6 +3,22 @@
 import jax.numpy as jnp
 from jax import lax
 from jax.sharding import PartitionSpec as P
+
+
+def swapped_with_each(array, axis, split, join):
+    ways, here = (lax.axis_size(axis), lax.axis_index(axis))
+    width = array.shape[split] // ways
+    dims = list(array.shape)
+    dims[split] = width
+    height = dims[join]
+    dims[join] = height * ways
+    full = jnp.zeros(dims, array.dtype)
+    for mask in range(ways):
+        part = lax.dynamic_slice_in_dim(array, (here ^ mask) * width, width, axis=split)
+        if mask:
+            part = lax.ppermute(part, axis, [(d, d ^ mask) for d in range(ways)])
+        full = lax.dynamic_update_slice_in_dim(full, part, (here ^ mask) * height, axis=join)
+    return full
 
 
 def extended(cells, sides, width):
@@ -82,12 +98,7 @@
         )
         rounded = rhs.astype(jnp.bfloat16)
         factors = 1.0 / (1.0 + step_size * (wall_rate[:, None] + span_part[None, :]))
-        solved = wall_solve(
-            lax.all_to_all(rounded, "gy", split_axis=2, concat_axis=1, tiled=True),
-            analysis,
-            synthesis,
-            factors,
-        )
+        solved = wall_solve(swapped_with_each(rounded, "gy", 2, 1), analysis, synthesis, factors)
         current = lax.all_to_all(solved, "gy", split_axis=1, concat_axis=2, tiled=True)
         if m < 2:
             new_explicit = explicit_term(current.astype(jnp.bfloat16)[None], velocity, decay_rate)[

time: 310 us -> 255 us (0.82)
  blocking collectives: 120 us -> 85.1 us
  local copies, waits for them, and re-layouts: 53.3 us -> 31.1 us
  other arithmetic: 32.4 us -> 18.8 us
  waiting for transfers between devices: 79.3 us -> 88.1 us
  starting transfers between devices: 12.7 us -> 20.8 us
    all_to_all x2 -> x0, blocking collectives: 36 us -> none  [per_device(): lax.all_to_all(rounded, 'gy', split_axis=2, concat_axis=1, tiled=True)]
    ppermute x0 -> x9, waiting for transfers between devices: none -> 20.4 us  [swapped_with_each(): part = lax.ppermute(part, axis, [(d, d ^ mask) for d in range(ways)])]
    unnamed x18 -> x8, local copies, waits for them, and re-layouts: 17.3 us -> 0.38 us
    unnamed x3 -> x0, other arithmetic: 13.6 us -> none
    ppermute x0 -> x9, starting transfers between devices: none -> 13.3 us  [swapped_with_each(): part = lax.ppermute(part, axis, [(d, d ^ mask) for d in range(ways)])]
    all_to_all x1 -> x0, waiting for transfers between devices: 11.3 us -> none  [per_device(): lax.all_to_all(rounded, 'gy', split_axis=2, concat_axis=1, tiled=True)]
    convert_element_type x3 -> x0, local copies, waits for them, and re-layouts: 7.18 us -> none  [per_device(): rounded = rhs.astype(jnp.bfloat16)]
    all_to_all x3 -> x0, local copies, waits for them, and re-layouts: 5.41 us -> none  [per_device(): lax.all_to_all(rounded, 'gy', split_axis=2, concat_axis=1, tiled=True)]
  transfers between devices with their start and end apart: 7 -> 15, of which waited for: 7 -> 11; matrix products, arithmetic and copies ran while one was open for 2% -> 4% of each run, Pallas kernels for 0% -> 0%
where the time goes in v1:
time: 255 us; the launch traced here: 254 us
  waiting for transfers between devices  88.1 us (35%)
  blocking collectives  85.1 us (33%)
  local copies, waits for them, and re-layouts  31.1 us (12%)
  starting transfers between devices  20.8 us (8%)
  other arithmetic  18.8 us (7%)
  matrix products  10.4 us (4%)
    all_to_all x3, blocking collectives, per_device(): lax.all_to_all(solved, 'gy', split_axis=1, concat_axis=2, tiled=True)  85.1 us
    ppermute x3, waiting for transfers between devices, extended(): lax.ppermute(head, axis, [((i + 1) % count, i) for i in range(count)])  58.9 us
    ppermute x9, waiting for transfers between devices, swapped_with_each(): part = lax.ppermute(part, axis, [(d, d ^ mask) for d in range(ways)])  20.4 us
    ppermute x9, starting transfers between devices, swapped_with_each(): part = lax.ppermute(part, axis, [(d, d ^ mask) for d in range(ways)])  13.3 us
    convert_element_type x3, other arithmetic, per_device(): rounded = rhs.astype(jnp.bfloat16)  10.9 us
    dot_general x3, matrix products, wall_solve(): jnp.einsum('ji,xik->xjk', synthesis, scaled, preferred_element_type=jnp.f...  10.4 us
    all_to_all x6, local copies, waits for them, and re-layouts, per_device(): lax.all_to_all(solved, 'gy', split_axis=1, concat_axis=2, tiled=True)  9 us
    ppermute x3, waiting for transfers between devices, extended(): lax.ppermute(tail, axis, [(i, (i + 1) % count) for i in range(count)])  8.82 us
  transfers between devices with their start and end apart: 15, of which 11 were waited for; matrix products, arithmetic and copies ran while one was open for 4% of the time, Pallas kernels for 0%

profile of v1, /device:TPU:0, one launch (start us, length us, event | category | flops | bytes accessed | tf_op | source)
XLA Modules:
  0.0 254.4 jit_solution(14871130868984471902)
XLA Ops:
  0.0 3.3 %collective-permute-start = (bf16[4,1,256,1024]{3,2,1,0:T(8,128)(2,1)}, bf16[4,1,256,1024]{3,2,1,0:T(8,128)(2,1)}, u32[]{:S(2)}, u32[]{:S(2)}) collective-permute-start(bf16[4,1,256,1024]{3,2,1,0:T(8,128)(2,1)} %param.8), channel_id=1, source_target_pairs={{4,0},{8,4},{12,8},{16,12},{20,16},{24,20},{28,24},{0,28},{5,1},{9... | collective-permute-start | bytes 6291464 | tf_op jit(solution)/shard_map/ppermute | solution.py:33
  4.0 44.7 %collective-permute-done = bf16[4,1,256,1024]{3,2,1,0:T(8,128)(2,1)} collective-permute-done((bf16[4,1,256,1024]{3,2,1,0:T(8,128)(2,1)}, bf16[4,1,256,1024]{3,2,1,0:T(8,128)(2,1)}, u32[]{:S(2)}, u32[]{:S(2)}) %collective-permute-start) | collective-permute-done | bytes 2097184 | tf_op jit(solution)/shard_map/ppermute | solution.py:33
  48.8 1.9 collective-permute-done.1
  50.7 5.7 %convert_add_fusion = (f32[4,1,256,1024]{3,2,1,0:T(8,128)S(1)}, f32[4,1,256,1024]{3,2,1,0:T(8,128)S(1)}) fusion(bf16[4,1,256,1024]{3,2,1,0:T(8,128)(2,1)} %param.9, bf16[4,1,256,1024]{3,2,1,0:T(8,128)(2,1)} %param.8, f32[256]{0:T(256)S(1)} %bitcast.143, bf16[4,1,256,1024]{3,2,1,0:T(8,128)(2,1)} %collective-permute-done.1, ...), kind=kLoop, calls=%fused_computation | loop fusion | flops 10485760 | bytes 16779264 | tf_op jit(solution)/shard_map/add | solution.py:85
  56.4 2.8 %fusion.29 = bf16[1,1,256,1024]{3,2,1,0:T(8,128)(2,1)S(1)} fusion(f32[4,1,256,1024]{3,2,1,0:T(8,128)S(1)} %get-tuple-element.6, f32[4,1,256,1024]{3,2,1,0:T(8,128)S(1)} %get-tuple-element.5, bf16[4,1,256,1024]{3,2,1,0:T(8,128)(2,1)} %param.9, bf16[4,1,256,1024]{3,2,1,0:T(8,128)(2,1)} %param.8), kind=kLoop, calls=%fused_computation.42 | loop fusion | flops 4194304 | bytes 6815744 | tf_op jit(solution)/shard_map/convert_element_type | solution.py:99
  62.0 2.6 %collective-permute-start.3 = (bf16[1,256,256]{2,1,0:T(8,128)(2,1)S(1)}, bf16[1,256,256]{2,1,0:T(8,128)(2,1)S(1)}, u32[]{:S(2)}, u32[]{:S(2)}) collective-permute-start(bf16[1,256,256]{2,1,0:T(8,128)(2,1)S(1)} %get-tuple-element.14), channel_id=1, source_target_pairs={{0,2},{1,3},{2,0},{3,1},{4,6},{5,7},{6,4},{7,5},{8,10},{9,11},{10,... | collective-permute-start | bytes 393224 | tf_op jit(solution)/shard_map/ppermute | solution.py:19
  67.0 5.4 %collective-permute-done.3 = bf16[1,256,256]{2,1,0:T(8,128)(2,1)S(1)} collective-permute-done((bf16[1,256,256]{2,1,0:T(8,128)(2,1)S(1)}, bf16[1,256,256]{2,1,0:T(8,128)(2,1)S(1)}, u32[]{:S(2)}, u32[]{:S(2)}) %collective-permute-start.3) | collective-permute-done | bytes 131104 | tf_op jit(solution)/shard_map/ppermute | solution.py:19
  73.7 3.2 %convolution_bitcast_fusion.4 = f32[1,1024,256]{1,2,0:T(8,128)S(1)} fusion(bf16[1024,1024]{1,0:T(8,128)(2,1)S(1)} %copy-done, bf16[1024,256]{1,0:T(8,128)(2,1)} %bitcast_dynamic-update-slice_fusion.8, bf16[1024,1024]{1,0:T(8,128)(2,1)} %param.14, f32[256]{0:T(256)S(1)} %dynamic_slice.51, f32[1024]{0:T(1024)S(1)} %copy-done.3), kind=kOutput, calls=%fused_computation.8 | convolution fusion | flops 1075314688 | bytes 5772288 | tf_op jit(solution)/shard_map/ji,xik->xjk/dot_general | solution.py:71
  76.9 1.9 copy.14
  78.8 27.0 %all_to_all.54 = f32[1,1024,256]{2,0,1:T(1,128)S(1)} all-to-all(f32[1,1024,256]{2,0,1:T(1,128)} %copy.14), channel_id=1, replica_groups=mesh['gx'=8,'gy'=4] {'gy'}, dimensions={1} | all-to-all | bytes 2097152 | tf_op jit(solution)/shard_map/all_to_all | solution.py:102
  108.0 2.3 convert_element_type.185
  110.2 3.7 %collective-permute-start.5 = (bf16[1,1,256,1024]{3,2,1,0:T(8,128)(2,1)}, bf16[1,1,256,1024]{3,2,1,0:T(8,128)(2,1)}, u32[]{:S(2)}, u32[]{:S(2)}) collective-permute-start(bf16[1,1,256,1024]{3,2,1,0:T(8,128)(2,1)} %convert_element_type.185), channel_id=1, source_target_pairs={{4,0},{8,4},{12,8},{16,12},{20,16},{24,20},{28,24},{0,28},{5,1},{9... | collective-permute-start | bytes 1572872 | tf_op jit(solution)/shard_map/ppermute | solution.py:33
  115.6 1.8 all_to_all.42
  117.3 7.4 %collective-permute-done.5 = bf16[1,1,256,1024]{3,2,1,0:T(8,128)(2,1)} collective-permute-done((bf16[1,1,256,1024]{3,2,1,0:T(8,128)(2,1)}, bf16[1,1,256,1024]{3,2,1,0:T(8,128)(2,1)}, u32[]{:S(2)}, u32[]{:S(2)}) %collective-permute-start.5) | collective-permute-done | bytes 524320 | tf_op jit(solution)/shard_map/ppermute | solution.py:33
  124.8 4.0 %collective-permute-done.6 = bf16[1,1,256,1024]{3,2,1,0:T(8,128)(2,1)} collective-permute-done((bf16[1,1,256,1024]{3,2,1,0:T(8,128)(2,1)}, bf16[1,1,256,1024]{3,2,1,0:T(8,128)(2,1)}, u32[]{:S(2)}, u32[]{:S(2)}) %collective-permute-start.6) | collective-permute-done | bytes 524320 | tf_op jit(solution)/shard_map/ppermute | solution.py:31
  128.8 4.1 %fusion.24 = bf16[1,256,1024]{2,1,0:T(8,128)(2,1)S(1)} fusion(f32[1,256,1024]{2,1,0:T(8,128)S(1)} %all_to_all.42, f32[4,1,256,1024]{3,2,1,0:T(8,128)} %copy-done.2, bf16[1,1,256,1024]{3,2,1,0:T(8,128)(2,1)} %convert_element_type.185, bf16[1,1,256,1024]{3,2,1,0:T(8,128)(2,1)} %collective-permute-done.6, bf16[1,1,256,1024]{3,2,1,0:T(8,128)(2,1)} %collective-permute-done.5, ...), kind=kLoop, calls=%fused_computation.36 | loop fusion | flops 6029312 | bytes 8914944 | tf_op jit(solution)/shard_map/convert_element_type | solution.py:99
  133.2 1.8 collective-permute-start.8
  135.0 2.4 collective-permute-start.9
  140.1 5.8 %collective-permute-done.8 = bf16[1,256,256]{2,1,0:T(8,128)(2,1)S(1)} collective-permute-done((bf16[1,256,256]{2,1,0:T(8,128)(2,1)S(1)}, bf16[1,256,256]{2,1,0:T(8,128)(2,1)S(1)}, u32[]{:S(2)}, u32[]{:S(2)}) %collective-permute-start.8) | collective-permute-done | bytes 131104 | tf_op jit(solution)/shard_map/ppermute | solution.py:19
  147.3 3.2 %convolution_bitcast_fusion.2 = f32[1,1024,256]{1,2,0:T(8,128)S(1)} fusion(bf16[1024,1024]{1,0:T(8,128)(2,1)S(1)} %copy-done, bf16[1024,256]{1,0:T(8,128)(2,1)} %bitcast_dynamic-update-slice_fusion.4, bf16[1024,1024]{1,0:T(8,128)(2,1)} %param.14, f32[256]{0:T(256)S(1)} %dynamic_slice.51, f32[1024]{0:T(1024)S(1)} %copy-done.3), kind=kOutput, calls=%fused_computation.6 | convolution fusion | flops 1075314688 | bytes 5772288 | tf_op jit(solution)/shard_map/ji,xik->xjk/dot_general | solution.py:71
  150.4 1.9 copy.17
  152.3 27.8 %all_to_all.55 = f32[1,1024,256]{2,0,1:T(1,128)S(1)} all-to-all(f32[1,1024,256]{2,0,1:T(1,128)} %copy.17), channel_id=1, replica_groups=mesh['gx'=8,'gy'=4] {'gy'}, dimensions={1} | all-to-all | bytes 2097152 | tf_op jit(solution)/shard_map/all_to_all | solution.py:102
  182.3 2.3 convert_element_type.193
  188.5 6.8 %collective-permute-done.10 = bf16[1,1,256,1024]{3,2,1,0:T(8,128)(2,1)} collective-permute-done((bf16[1,1,256,1024]{3,2,1,0:T(8,128)(2,1)}, bf16[1,1,256,1024]{3,2,1,0:T(8,128)(2,1)}, u32[]{:S(2)}, u32[]{:S(2)}) %collective-permute-start.10) | collective-permute-done | bytes 524320 | tf_op jit(solution)/shard_map/ppermute | solution.py:33
  195.3 2.9 %collective-permute-done.11 = bf16[1,1,256,1024]{3,2,1,0:T(8,128)(2,1)} collective-permute-done((bf16[1,1,256,1024]{3,2,1,0:T(8,128)(2,1)}, bf16[1,1,256,1024]{3,2,1,0:T(8,128)(2,1)}, u32[]{:S(2)}, u32[]{:S(2)}) %collective-permute-start.11) | collective-permute-done | bytes 524320 | tf_op jit(solution)/shard_map/ppermute | solution.py:31
  198.1 4.1 %fusion.18 = bf16[1,256,1024]{2,1,0:T(8,128)(2,1)S(1)} fusion(f32[1,256,1024]{2,1,0:T(8,128)S(1)} %all_to_all.46, f32[4,1,256,1024]{3,2,1,0:T(8,128)} %copy-done.2, bf16[1,1,256,1024]{3,2,1,0:T(8,128)(2,1)} %convert_element_type.193, bf16[1,1,256,1024]{3,2,1,0:T(8,128)(2,1)} %collective-permute-done.11, ...), kind=kLoop, calls=%fused_computation.29 | loop fusion | flops 6029312 | bytes 8914944 | tf_op jit(solution)/shard_map/convert_element_type | solution.py:99
  204.3 2.4 collective-permute-start.14
  206.8 3.1 %collective-permute-done.12 = bf16[1,256,256]{2,1,0:T(8,128)(2,1)S(1)} collective-permute-done((bf16[1,256,256]{2,1,0:T(8,128)(2,1)S(1)}, bf16[1,256,256]{2,1,0:T(8,128)(2,1)S(1)}, u32[]{:S(2)}, u32[]{:S(2)}) %collective-permute-start.12) | collective-permute-done | bytes 131104 | tf_op jit(solution)/shard_map/ppermute | solution.py:19
  209.9 5.5 %collective-permute-done.13 = bf16[1,256,256]{2,1,0:T(8,128)(2,1)S(1)} collective-permute-done((bf16[1,256,256]{2,1,0:T(8,128)(2,1)S(1)}, bf16[1,256,256]{2,1,0:T(8,128)(2,1)S(1)}, u32[]{:S(2)}, u32[]{:S(2)}) %collective-permute-start.13) | collective-permute-done | bytes 131104 | tf_op jit(solution)/shard_map/ppermute | solution.py:19
  215.5 4.0 %convolution_bitcast_fusion = f32[1,1024,256]{1,2,0:T(8,128)} fusion(bf16[1024,1024]{1,0:T(8,128)(2,1)S(1)} %copy-done, bf16[1024,256]{1,0:T(8,128)(2,1)S(1)} %bitcast_dynamic-update-slice_fusion, bf16[1024,1024]{1,0:T(8,128)(2,1)} %param.14, f32[256]{0:T(256)S(1)} %dynamic_slice.51, f32[1024]{0:T(1024)S(1)} %copy-done.3), kind=kOutput, calls=%fused_computation.4 | convolution fusion | flops 1075314688 | bytes 5772288 | tf_op jit(solution)/shard_map/ji,xik->xjk/dot_general | solution.py:71
  219.5 2.4 copy.20
  221.9 30.3 %all_to_all.56 = f32[1,1024,256]{2,0,1:T(1,128)S(1)} all-to-all(f32[1,1024,256]{2,0,1:T(1,128)S(1)} %copy.20), channel_id=1, replica_groups=mesh['gx'=8,'gy'=4] {'gy'}, dimensions={1} | all-to-all | bytes 2097152 | tf_op jit(solution)/shard_map/all_to_all | solution.py:102
  (51 shorter events, 25.9 us)
Async XLA Ops:
  0.0 73.7 %copy-start = (bf16[1024,1024]{1,0:T(8,128)(2,1)S(1)}, bf16[1024,1024]{1,0:T(8,128)(2,1)}, u32[]{:S(2)}) copy-start(bf16[1024,1024]{1,0:T(8,128)(2,1)} %param.15) | copy-start | bytes 6291460
  0.0 48.8 %collective-permute-start = (bf16[4,1,256,1024]{3,2,1,0:T(8,128)(2,1)}, bf16[4,1,256,1024]{3,2,1,0:T(8,128)(2,1)}, u32[]{:S(2)}, u32[]{:S(2)}) collective-permute-start(bf16[4,1,256,1024]{3,2,1,0:T(8,128)(2,1)} %param.8), channel_id=1, source_target_pairs={{4,0},{8,4},{12,8},{16,12},{20,16},{24,20},{28,24},{0,28},{5,1},{9... | collective-permute-start | bytes 6291464 | tf_op jit(solution)/shard_map/ppermute | solution.py:33
  3.3 47.4 %collective-permute-start.1 = (bf16[4,1,256,1024]{3,2,1,0:T(8,128)(2,1)}, bf16[4,1,256,1024]{3,2,1,0:T(8,128)(2,1)}, u32[]{:S(2)}, u32[]{:S(2)}) collective-permute-start(bf16[4,1,256,1024]{3,2,1,0:T(8,128)(2,1)} %param.8), channel_id=1, source_target_pairs={{0,4},{4,8},{8,12},{12,16},{16,20},{20,24},{24,28},{28,0},{1,5},{5... | collective-permute-start | bytes 6291464 | tf_op jit(solution)/shard_map/ppermute | solution.py:31
  56.4 2.8 %copy-start.1 = (f32[4,1,256,1024]{3,2,1,0:T(8,128)}, f32[4,1,256,1024]{3,2,1,0:T(8,128)S(1)}, u32[]{:S(2)}) copy-start(f32[4,1,256,1024]{3,2,1,0:T(8,128)S(1)} %get-tuple-element.5) | copy-start | bytes 12582916
  56.4 3.3 %copy-start.2 = (f32[4,1,256,1024]{3,2,1,0:T(8,128)}, f32[4,1,256,1024]{3,2,1,0:T(8,128)S(1)}, u32[]{:S(2)}) copy-start(f32[4,1,256,1024]{3,2,1,0:T(8,128)S(1)} %get-tuple-element.6) | copy-start | bytes 12582916
  59.2 14.5 %copy-start.3 = (f32[1024]{0:T(1024)S(1)}, f32[1024]{0:T(1024)}, u32[]{:S(2)}) copy-start(f32[1024]{0:T(1024)} %param.12) | copy-start | bytes 12292
  59.7 6.7 %collective-permute-start.2 = (bf16[1,256,256]{2,1,0:T(8,128)(2,1)S(1)}, bf16[1,256,256]{2,1,0:T(8,128)(2,1)S(1)}, u32[]{:S(2)}, u32[]{:S(2)}) collective-permute-start(bf16[1,256,256]{2,1,0:T(8,128)(2,1)S(1)} %get-tuple-element.15), channel_id=1, source_target_pairs={{0,1},{1,0},{2,3},{3,2},{4,5},{5,4},{6,7},{7,6},{8,9},{9,8},{10,11... | collective-permute-start | bytes 393224 | tf_op jit(solution)/shard_map/ppermute | solution.py:19
  62.0 10.4 %collective-permute-start.3 = (bf16[1,256,256]{2,1,0:T(8,128)(2,1)S(1)}, bf16[1,256,256]{2,1,0:T(8,128)(2,1)S(1)}, u32[]{:S(2)}, u32[]{:S(2)}) collective-permute-start(bf16[1,256,256]{2,1,0:T(8,128)(2,1)S(1)} %get-tuple-element.14), channel_id=1, source_target_pairs={{0,2},{1,3},{2,0},{3,1},{4,6},{5,7},{6,4},{7,5},{8,10},{9,11},{10,... | collective-permute-start | bytes 393224 | tf_op jit(solution)/shard_map/ppermute | solution.py:19
  64.6 8.4 %collective-permute-start.4 = (bf16[1,256,256]{2,1,0:T(8,128)(2,1)S(1)}, bf16[1,256,256]{2,1,0:T(8,128)(2,1)S(1)}, u32[]{:S(2)}, u32[]{:S(2)}) collective-permute-start(bf16[1,256,256]{2,1,0:T(8,128)(2,1)S(1)} %get-tuple-element.13), channel_id=1, source_target_pairs={{0,3},{1,2},{2,1},{3,0},{4,7},{5,6},{6,5},{7,4},{8,11},{9,10},{10,... | collective-permute-start | bytes 393224 | tf_op jit(solution)/shard_map/ppermute | solution.py:19
  110.2 14.5 %collective-permute-start.5 = (bf16[1,1,256,1024]{3,2,1,0:T(8,128)(2,1)}, bf16[1,1,256,1024]{3,2,1,0:T(8,128)(2,1)}, u32[]{:S(2)}, u32[]{:S(2)}) collective-permute-start(bf16[1,1,256,1024]{3,2,1,0:T(8,128)(2,1)} %convert_element_type.185), channel_id=1, source_target_pairs={{4,0},{8,4},{12,8},{16,12},{20,16},{24,20},{28,24},{0,28},{5,1},{9... | collective-permute-start | bytes 1572872 | tf_op jit(solution)/shard_map/ppermute | solution.py:33
  113.9 14.9 %collective-permute-start.6 = (bf16[1,1,256,1024]{3,2,1,0:T(8,128)(2,1)}, bf16[1,1,256,1024]{3,2,1,0:T(8,128)(2,1)}, u32[]{:S(2)}, u32[]{:S(2)}) collective-permute-start(bf16[1,1,256,1024]{3,2,1,0:T(8,128)(2,1)} %convert_element_type.185), channel_id=1, source_target_pairs={{0,4},{4,8},{8,12},{12,16},{16,20},{20,24},{24,28},{28,0},{1,5},{5... | collective-permute-start | bytes 1572872 | tf_op jit(solution)/shard_map/ppermute | solution.py:31
  132.9 6.5 %collective-permute-start.7 = (bf16[1,256,256]{2,1,0:T(8,128)(2,1)S(1)}, bf16[1,256,256]{2,1,0:T(8,128)(2,1)S(1)}, u32[]{:S(2)}, u32[]{:S(2)}) collective-permute-start(bf16[1,256,256]{2,1,0:T(8,128)(2,1)S(1)} %get-tuple-element.12), channel_id=1, source_target_pairs={{0,1},{1,0},{2,3},{3,2},{4,5},{5,4},{6,7},{7,6},{8,9},{9,8},{10,11... | collective-permute-start | bytes 393224 | tf_op jit(solution)/shard_map/ppermute | solution.py:19
  133.2 12.7 %collective-permute-start.8 = (bf16[1,256,256]{2,1,0:T(8,128)(2,1)S(1)}, bf16[1,256,256]{2,1,0:T(8,128)(2,1)S(1)}, u32[]{:S(2)}, u32[]{:S(2)}) collective-permute-start(bf16[1,256,256]{2,1,0:T(8,128)(2,1)S(1)} %get-tuple-element.11), channel_id=1, source_target_pairs={{0,2},{1,3},{2,0},{3,1},{4,6},{5,7},{6,4},{7,5},{8,10},{9,11},{10,... | collective-permute-start | bytes 393224 | tf_op jit(solution)/shard_map/ppermute | solution.py:19
  135.0 11.6 %collective-permute-start.9 = (bf16[1,256,256]{2,1,0:T(8,128)(2,1)S(1)}, bf16[1,256,256]{2,1,0:T(8,128)(2,1)S(1)}, u32[]{:S(2)}, u32[]{:S(2)}) collective-permute-start(bf16[1,256,256]{2,1,0:T(8,128)(2,1)S(1)} %get-tuple-element.10), channel_id=1, source_target_pairs={{0,3},{1,2},{2,1},{3,0},{4,7},{5,6},{6,5},{7,4},{8,11},{9,10},{10,... | collective-permute-start | bytes 393224 | tf_op jit(solution)/shard_map/ppermute | solution.py:19
  184.6 10.7 %collective-permute-start.10 = (bf16[1,1,256,1024]{3,2,1,0:T(8,128)(2,1)}, bf16[1,1,256,1024]{3,2,1,0:T(8,128)(2,1)}, u32[]{:S(2)}, u32[]{:S(2)}) collective-permute-start(bf16[1,1,256,1024]{3,2,1,0:T(8,128)(2,1)} %convert_element_type.193), channel_id=1, source_target_pairs={{4,0},{8,4},{12,8},{16,12},{20,16},{24,20},{28,24},{0,28},{5,1},{9... | collective-permute-start | bytes 1572872 | tf_op jit(solution)/shard_map/ppermute | solution.py:33
  184.6 13.5 %collective-permute-start.11 = (bf16[1,1,256,1024]{3,2,1,0:T(8,128)(2,1)}, bf16[1,1,256,1024]{3,2,1,0:T(8,128)(2,1)}, u32[]{:S(2)}, u32[]{:S(2)}) collective-permute-start(bf16[1,1,256,1024]{3,2,1,0:T(8,128)(2,1)} %convert_element_type.193), channel_id=1, source_target_pairs={{0,4},{4,8},{8,12},{12,16},{16,20},{20,24},{24,28},{28,0},{1,5},{5... | collective-permute-start | bytes 1572872 | tf_op jit(solution)/shard_map/ppermute | solution.py:31
  202.3 7.7 %collective-permute-start.12 = (bf16[1,256,256]{2,1,0:T(8,128)(2,1)S(1)}, bf16[1,256,256]{2,1,0:T(8,128)(2,1)S(1)}, u32[]{:S(2)}, u32[]{:S(2)}) collective-permute-start(bf16[1,256,256]{2,1,0:T(8,128)(2,1)S(1)} %get-tuple-element.9), channel_id=1, source_target_pairs={{0,1},{1,0},{2,3},{3,2},{4,5},{5,4},{6,7},{7,6},{8,9},{9,8},{10,11... | collective-permute-start | bytes 393224 | tf_op jit(solution)/shard_map/ppermute | solution.py:19
  202.5 12.9 %collective-permute-start.13 = (bf16[1,256,256]{2,1,0:T(8,128)(2,1)S(1)}, bf16[1,256,256]{2,1,0:T(8,128)(2,1)S(1)}, u32[]{:S(2)}, u32[]{:S(2)}) collective-permute-start(bf16[1,256,256]{2,1,0:T(8,128)(2,1)S(1)} %get-tuple-element.8), channel_id=1, source_target_pairs={{0,2},{1,3},{2,0},{3,1},{4,6},{5,7},{6,4},{7,5},{8,10},{9,11},{10,... | collective-permute-start | bytes 393224 | tf_op jit(solution)/shard_map/ppermute | solution.py:19
  204.3 11.2 %collective-permute-start.14 = (bf16[1,256,256]{2,1,0:T(8,128)(2,1)S(1)}, bf16[1,256,256]{2,1,0:T(8,128)(2,1)S(1)}, u32[]{:S(2)}, u32[]{:S(2)}) collective-permute-start(bf16[1,256,256]{2,1,0:T(8,128)(2,1)S(1)} %get-tuple-element.7), channel_id=1, source_target_pairs={{0,3},{1,2},{2,1},{3,0},{4,7},{5,6},{6,5},{7,4},{8,11},{9,10},{10,... | collective-permute-start | bytes 393224 | tf_op jit(solution)/shard_map/ppermute | solution.py:19
